TPU v7x, 32 devices: a whole 2x2x4 slice. The times are simulated.
32 devices in a mesh: groups: 2 (over x), tp: 16 (over z, y, core).
Axes of the slice: x: 2, y: 2, z: 4, core: 2. Of those that a mesh axis runs over, the one named last changes fastest.
Arguments:
- hidden: bfloat16 [1536, 28672], P('groups', 'tp'), parts along dimension 0, may hold values from -6 to 6
- positions: int32 [768], P('groups'), parts along dimension 0, may hold values from 0 to 767, as said below
- adapter_rows: int32 [28672], P('tp'), may hold values from 0 to 28671, as said below
- adapter_a: bfloat16 [28672, 64], P('tp'), may hold values from -1 to 1
- adapter_b: bfloat16 [64, 8192], P(None, 'tp'), may hold values from -0.03125 to 0.03125
- frozen_down_weight: bfloat16 [28672, 8192], P('tp'), may hold values from -0.03125 to 0.03125
- residual: bfloat16 [768, 8192], P(('groups', 'tp')), parts along dimension 0, may hold values from -6 to 6
- gain: bfloat16 [8192], replicated, may hold values from 0.099609375 to 1.8984375
Outputs:
- normed: bfloat16 [768, 8192], P('groups'), parts along dimension 0
There are 2 independent parts, one for each index of `groups`. A program takes and returns all parts, laid end to end along the dimension named above; an argument that names none is the same for every part. Nothing has to cross between parts.
Inputs may be any that keep to these rules, and one draw needn't show every extreme that they name: `adapter_rows`: A permutation of the row numbers. Of the 1792 entries in each aligned block of 1792 positions, at most 224 lie in any one aligned block of 1792 row numbers, and every block of positions has exactly 224 in one block of row numbers. `positions`: Distinct.
All inputs are finite; a program needn't handle non-finite values.
Results may differ from a plain program's by a relative error of at most 0.013.
Values may be sent and summed in bfloat16 or wider, within the bound.
A program may use at most 128 MiB of HBM per device.

v0:
```python
import jax
import jax.numpy as jnp
from jax import lax
from jax.sharding import PartitionSpec as P

adapter_scale = 2.0
norm_eps = 1e-05


def normalize(residual_rows, summed, gain):
    stream = residual_rows.astype(jnp.float32) + summed
    inverse_rms = lax.rsqrt(jnp.mean(stream * stream, axis=-1, keepdims=True) + norm_eps)
    return (stream * inverse_rms * gain.astype(jnp.float32)).astype(jnp.bfloat16)


def on_device(
    hidden, positions, adapter_rows, adapter_a, adapter_b, frozen_down_weight, residual, gain
):
    group_size = lax.axis_size("tp")
    own_rows = frozen_down_weight.shape[0]
    adapter_inner_rank = adapter_a.shape[1]
    first_row = lax.axis_index("tp") * own_rows
    capacity = 2 * own_rows // group_size
    owners = adapter_rows // own_rows
    onehot = (owners[:, None] == jnp.arange(group_size, dtype=jnp.int32)[None, :]).astype(jnp.int32)
    slot_rank = jnp.sum((jnp.cumsum(onehot, axis=0) - onehot) * onehot, axis=1)
    slot_index = owners * capacity + slot_rank
    send_rows = (
        jnp.zeros((group_size * capacity, adapter_inner_rank), adapter_a.dtype)
        .at[slot_index]
        .set(adapter_a)
    )
    send_ids = jnp.full((group_size * capacity,), -1, jnp.int32).at[slot_index].set(adapter_rows)
    got_rows, got_ids = (
        lax.all_to_all(send_rows, "tp", split_axis=0, concat_axis=0, tiled=True),
        lax.all_to_all(send_ids, "tp", split_axis=0, concat_axis=0, tiled=True),
    )
    local_row = got_ids - first_row
    is_mine = (local_row >= 0) & (local_row < own_rows)
    target = jnp.where(is_mine, local_row, own_rows)
    factor_a = (
        jnp.zeros((own_rows, adapter_inner_rank), adapter_a.dtype)
        .at[target]
        .set(got_rows, mode="drop")
    )
    low_rank_update = jnp.dot(
        factor_a,
        lax.all_gather(adapter_b, "tp", axis=1, tiled=True),
        preferred_element_type=jnp.float32,
    )
    merged_weight = (
        frozen_down_weight.astype(jnp.float32) + adapter_scale * low_rank_update
    ).astype(frozen_down_weight.dtype)
    late_rows = jnp.take(hidden, positions, axis=0)
    summed = lax.psum_scatter(
        jnp.dot(late_rows, merged_weight, preferred_element_type=jnp.float32).astype(jnp.bfloat16),
        "tp",
        scatter_dimension=0,
        tiled=True,
    ).astype(jnp.float32)
    normed = normalize(residual, summed, gain)
    return lax.all_gather(normed, "tp", axis=0, tiled=True)


def solution(mesh):
    placed = (
        P("groups", "tp"),
        P("groups"),
        P("tp"),
        P("tp", None),
        P(None, "tp"),
        P("tp", None),
        P(("groups", "tp"), None),
        P(),
    )
    return jax.shard_map(
        on_device, mesh=mesh, in_specs=placed, out_specs=P("groups", None), check_vma=False
    )
```

profile of v0, /device:TPU:29, one launch (start us, length us, event | category | flops | bytes accessed | tf_op | source)
XLA Modules:
  0.0 258.2 jit_solution(17009375153558616787)
XLA Ops:
  6.5 0.0 copy-start
  6.5 0.0 all-gather.3.cloned.1.call-start
  6.5 0.7 all-gather.3.cloned.1.call-update
  7.3 0.8 add_select_fusion
  8.1 4.5 %reduce-window.6 = s32[16,14,128]{2,1,0:T(8,128)S(1)} reduce-window(s32[16,14,128]{2,1,0:T(8,128)S(1)} %fusion.7, s32[]{:T(128)} %constant.15.clone.1), window={size=1x1x128 pad=0_0x0_0x127_0}, to_apply=%region_0.1 | reduce-window | flops 3641344 | bytes 229380 | tf_op jit(solution)/shard_map/reduce-window
  12.6 0.4 slice_reduce_fusion
  13.1 0.2 reduce-window.9
  13.2 0.1 broadcast_add_fusion
  13.4 0.1 fusion.10
  13.4 0.7 compare_select_fusion.1
  14.1 7.3 %scatter_custom_fusion = s32[3584]{0:T(1024)S(1)} fusion(s32[1792]{0:T(1024)S(1)} %compare_select_fusion.1, s32[1792]{0:T(1024)} %param.10, s32[]{:T(128)} %constant.23.clone.1), kind=kCustom, calls=%fused_computation.33 | custom fusion | bytes 14848 | tf_op jit(solution)/shard_map/scatter | solution.py:33
  21.4 0.7 all_to_all.19
  22.1 6.3 %all-to-all-start = ((s32[16,224,1]{1,2,0:T(1,128)}), s32[16,224,1]{1,2,0:T(1,128)S(1)}, u32[]{:S(2)}, u32[]{:S(2)}) async-start(s32[16,224,1]{1,2,0:T(1,128)} %all_to_all.19), calls=%async_computation | async-start | bytes 32768 | tf_op jit(solution)/shard_map/all_to_all | solution.py:36
  28.5 1.2 copy.18
  29.7 9.1 %scatter_custom_fusion.1 = bf16[3584,64]{1,0:T(8,128)(2,1)} fusion(s32[1792]{0:T(1024)S(1)} %compare_select_fusion.1, bf16[1792,64]{1,0:T(8,128)(2,1)S(1)} %copy.18, bf16[]{:T(256)} %constant.22.clone.1), kind=kCustom, calls=%fused_computation.12 | custom fusion | bytes 458754 | tf_op jit(solution)/shard_map/scatter | solution.py:31
  38.8 2.3 copy.19
  41.1 0.0 all-to-all-done
  41.1 6.0 %all-to-all-start.1 = ((bf16[16,224,64]{1,2,0:T(8,128)(2,1)}), bf16[16,224,64]{1,2,0:T(8,128)(2,1)S(1)}, u32[]{:S(2)}, u32[]{:S(2)}) async-start(bf16[16,224,64]{1,2,0:T(8,128)(2,1)} %copy.19), calls=%async_computation.1 | async-start | bytes 1048576 | tf_op jit(solution)/shard_map/all_to_all | solution.py:35
  47.1 0.0 copy-start.3
  47.1 0.0 reduce-scatter.2.cloned.1.call-start
  47.1 0.7 compare_select_fusion.2
  47.8 0.0 copy-done
  47.8 3.0 %gather_fusion = bf16[384,1792]{1,0:T(8,128)(2,1)} fusion(bf16[768,1792]{1,0:T(8,128)(2,1)S(1)} %copy-done, s32[1024]{0:T(1024)S(1)} %pad_clamp_fusion), kind=kCustom, calls=%fused_computation | custom fusion | bytes 2754048 | tf_op jit(solution)/shard_map/jit(_take)/gather | solution.py:54
  50.8 0.0 copy-done.3
  50.9 0.1 sub.29
  51.0 0.1 fusion.11
  51.1 8.7 %all-to-all-done.1 = bf16[16,224,64]{1,2,0:T(8,128)(2,1)S(1)} async-done(((bf16[16,224,64]{1,2,0:T(8,128)(2,1)}), bf16[16,224,64]{1,2,0:T(8,128)(2,1)S(1)}, u32[]{:S(2)}, u32[]{:S(2)}) %all-to-all-start.1) | async-done | bytes 458784 | tf_op jit(solution)/shard_map/all_to_all | solution.py:35
  59.8 1.2 copy.22
  61.0 10.1 %scatter_custom_fusion.2 = bf16[1792,64]{1,0:T(8,128)(2,1)S(1)} fusion(s32[3584]{0:T(1024)S(1)} %fusion.11, bf16[3584,64]{1,0:T(8,128)(2,1)} %bitcast.28, bf16[]{:T(256)} %constant.22.clone.1), kind=kCustom, calls=%fused_computation.14 | custom fusion | bytes 229888 | tf_op jit(solution)/shard_map/scatter | solution.py:44
  71.2 0.0 all-gather.3.cloned.1.call-done
  71.2 26.0 %convolution_convert_fusion = bf16[384,8192]{1,0:T(8,128)(2,1)} fusion(bf16[1792,8192]{1,0:T(8,128)(2,1)} %param.13, bf16[1792,64]{1,0:T(8,128)(2,1)S(1)} %scatter_custom_fusion.2, bf16[64,8192]{1,0:T(8,128)(2,1)} %all-gather.3.cloned.1.call-done, bf16[384,1792]{1,0:T(8,128)(2,1)} %gather_fusion, pred[384]{0:T(512)(128)(4,1)S(1)} %compare_and_fusion), kind=kOutput, calls=%fused_computation.5 | convolution fusion | flops 13215891456 | bytes 38306176 | tf_op jit(solution)/shard_map/dot_general | solution.py:56
  97.2 0.0 copy-start.2
  97.2 0.0 copy-start.1
  97.2 0.0 reduce-scatter.2.cloned.1.call-update
  97.2 0.0 all-gather.5.cloned.1.call-start
  97.3 0.6 copy-done.2
  97.9 83.1 %reduce-scatter.2.cloned.1.call-done = bf16[24,8192]{1,0:T(8,128)(2,1)} async-done(((bf16[384,8192]{1,0:T(8,128)(2,1)}), bf16[24,8192]{1,0:T(8,128)(2,1)}) %reduce-scatter.2.cloned.1.call-update) | async-done | bytes 393232 | tf_op jit(solution)/shard_map/reduce_scatter | solution.py:55
  181.0 0.0 copy-done.1
  181.0 1.2 multiply_reduce_fusion
  182.3 1.9 multiply_convert_fusion
  184.2 0.0 all-gather.5.cloned.1.call-update
  184.2 61.3 %all-gather.5.cloned.1.call-done = bf16[384,8192]{1,0:T(8,128)(2,1)} async-done(((bf16[24,8192]{1,0:T(8,128)(2,1)}), bf16[384,8192]{1,0:T(8,128)(2,1)}) %all-gather.5.cloned.1.call-update) | async-done | bytes 6291472 | tf_op jit(solution)/shard_map/all_gather | solution.py:62
  245.5 6.2 %copy.27 = bf16[384,8192]{1,0:T(8,128)(2,1)} copy(bf16[384,8192]{1,0:T(8,128)(2,1)} %all-gather.5.cloned.1.call-done) | data formatting | bytes 12582912
  (6 shorter events, 0.1 us)
Async XLA Ops:
  6.5 41.3 %copy-start = (bf16[768,1792]{1,0:T(8,128)(2,1)S(1)}, bf16[768,1792]{1,0:T(8,128)(2,1)}, u32[]{:S(2)}) copy-start(bf16[768,1792]{1,0:T(8,128)(2,1)} %param.8) | copy-start | bytes 8257540
  6.5 64.7 %all-gather.3.cloned.1.call-start = ((), (), s32[]{:S(2)}) async-start(), calls=%async_computation.3 | async-start | bytes 1114112 | tf_op jit(solution)/shard_map/all_gather | solution.py:48
  22.1 19.0 %all-to-all-start = ((s32[16,224,1]{1,2,0:T(1,128)}), s32[16,224,1]{1,2,0:T(1,128)S(1)}, u32[]{:S(2)}, u32[]{:S(2)}) async-start(s32[16,224,1]{1,2,0:T(1,128)} %all_to_all.19), calls=%async_computation | async-start | bytes 32768 | tf_op jit(solution)/shard_map/all_to_all | solution.py:36
  41.1 18.7 %all-to-all-start.1 = ((bf16[16,224,64]{1,2,0:T(8,128)(2,1)}), bf16[16,224,64]{1,2,0:T(8,128)(2,1)S(1)}, u32[]{:S(2)}, u32[]{:S(2)}) async-start(bf16[16,224,64]{1,2,0:T(8,128)(2,1)} %copy.19), calls=%async_computation.1 | async-start | bytes 1048576 | tf_op jit(solution)/shard_map/all_to_all | solution.py:35
  47.1 3.8 %copy-start.3 = (s32[384]{0:T(512)S(1)}, s32[384]{0:T(512)}, u32[]{:S(2)}) copy-start(s32[384]{0:T(512)} %param.9) | copy-start | bytes 4612
  47.1 134.0 %reduce-scatter.2.cloned.1.call-start = ((), (), s32[]{:S(2)}) async-start(), calls=%async_computation.4 | async-start | bytes 6684672 | tf_op jit(solution)/shard_map/reduce_scatter | solution.py:55
  97.2 0.7 copy-start.2
  97.2 83.9 %copy-start.1 = (bf16[24,8192]{1,0:T(8,128)(2,1)S(1)}, bf16[24,8192]{1,0:T(8,128)(2,1)}, u32[]{:S(2)}) copy-start(bf16[24,8192]{1,0:T(8,128)(2,1)} %param.14) | copy-start | bytes 1179652
  97.2 148.3 %all-gather.5.cloned.1.call-start = ((), (), s32[]{:S(2)}) async-start(), calls=%async_computation.5 | async-start | bytes 6684672 | tf_op jit(solution)/shard_map/all_gather | solution.py:62
Sparse Core Ops, SparseCore 0:
  9.5 36.7 all-gather.2
  97.3 83.6 reduce-scatter.1
  184.3 61.1 all-gather.4
where the time goes:
time: 262 us; the launch traced here: 258 us
  waiting for transfers between devices  154 us (59%)
  local copies, waits for them, and re-layouts  42.4 us (16%)
  matrix products  26 us (10%)
  between operations  13.2 us (5%)
  starting transfers between devices  12.4 us (5%)
  other arithmetic  10.4 us (4%)
    reduce_scatter x1, waiting for transfers between devices, on_device(): lax.psum_scatter(jnp.dot(late_rows, merged_weight, preferred_element_type...  83.1 us
    all_gather x1, waiting for transfers between devices, on_device(): return lax.all_gather(normed, 'tp', axis=0, tiled=True)  61.3 us
    dot_general x1, matrix products, on_device(): jnp.dot(late_rows, merged_weight, preferred_element_type=jnp.float32)  26 us
    scatter x1, local copies, waits for them, and re-layouts, on_device(): factor_a = jnp.zeros((own_rows, adapter_inner_rank), adapter_a.dtype).at[...  10.1 us
    scatter x1, local copies, waits for them, and re-layouts, on_device(): send_rows = jnp.zeros((group_size * capacity, adapter_inner_rank), adapte...  9.09 us
    all_to_all x1, waiting for transfers between devices, on_device(): lax.all_to_all(send_rows, 'tp', split_axis=0, concat_axis=0, tiled=True)  8.7 us
    unnamed x10, local copies, waits for them, and re-layouts  8.05 us
    scatter x1, local copies, waits for them, and re-layouts, on_device(): jnp.full((group_size * capacity,), -1, jnp.int32).at[slot_index]  7.29 us
  transfers between devices with their start and end apart: 5, of which 3 were waited for; matrix products, arithmetic and copies ran while one was open for 16% of the time, Pallas kernels for 0%

commit v1 on v0

v1 whole, which is shorter than its diff:
```python
import functools

import jax
import jax.numpy as jnp
from jax import lax
from jax.experimental import pallas as pl
from jax.experimental.pallas import tpu as pltpu
from jax.sharding import PartitionSpec as P

adapter_scale = 2.0
norm_eps = 1e-05
CHUNKS = 8
PIECES = 4
W_SLOTS = 3
BF16 = jnp.bfloat16
F32 = jnp.float32
NT = (((1,), (1,)), ((), ()))


def kernel(
    cfg,
    pos_ref, hidden_ref, ids_ref, aa_ref, b_ref, w_hbm, res_ref, gain_ref,
    out_hbm,
    wbuf, late, code, idrows, abuf, got, uacc, tsend, trecv, bfull,
    pbuf, c_send, c_recv, y_send, y_recv, y_own, z_send, z_recv, stream, nbuf,
    w_sem, cs, cr, ys, yr, zs, zr, as_, ar, ts, tr,
    bzs, bzr, bys, byr, bcs, bcr, gzs, gzr, gys, gyr, gcs, gcr, loc,
):
    tp, nz, rows, tokens, half, hp, own_rows, d_model = cfg
    n = CHUNKS
    hd = d_model // 2
    cw = hd // n
    me = lax.axis_index("tp")
    z, y, c = me // 4, (me // 2) % 2, me % 2
    sib = me + 1 - 2 * c
    ypeer = me + 2 - 4 * y
    nb = 2 * nz

    def remote(src, dst, send, recv, dev):
        return pltpu.make_async_remote_copy(
            src_ref=src, dst_ref=dst, send_sem=send, recv_sem=recv,
            device_id={"tp": dev}, device_id_type=pl.DeviceIdType.MESH,
        )

    def w_copies(j):
        slot = lax.rem(j, W_SLOTS)
        return [
            pltpu.make_async_copy(
                w_hbm.at[:, pl.ds(pl.multiple_of(h * hd + j * cw, 128), cw)],
                wbuf.at[slot, :, pl.ds(h * cw, cw)],
                w_sem.at[slot, h],
            )
            for h in range(2)
        ]

    for j in range(W_SLOTS - 1):
        for copy in w_copies(j):
            copy.start()

    barrier = pltpu.get_barrier_semaphore()

    @pl.loop(1, tp)
    def _(i):
        pl.semaphore_signal(
            barrier, inc=1, device_id={"tp": lax.rem(me + i, tp)},
            device_id_type=pl.DeviceIdType.MESH,
        )

    buf_rows = hidden_ref.shape[0]
    pick = jnp.where(
        pos_ref[...] == lax.broadcasted_iota(jnp.int32, (tokens, buf_rows), 1), 1.0, 0.0
    ).astype(BF16)
    lw = 256 if own_rows % 256 == 0 else 128
    for t in range(own_rows // lw):
        late[:, t * lw : (t + 1) * lw] = jnp.dot(
            pick, hidden_ref[:, t * lw : (t + 1) * lw], preferred_element_type=F32
        ).astype(BF16)

    ids = ids_ref[...]
    first = lax.broadcasted_iota(jnp.int32, (tp, 1), 0) * own_rows
    mine = (ids >= first) & (ids < first + own_rows)
    hot = jnp.where(mine, 1.0, 0.0)
    local = jnp.sum(jnp.where(mine, ids - first, 0), axis=0, keepdims=True)
    before = jnp.where(
        lax.broadcasted_iota(jnp.int32, (128, 128), 0)
        < lax.broadcasted_iota(jnp.int32, (128, 128), 1), 1.0, 0.0,
    ).astype(BF16)
    carry = jnp.zeros((tp, 1), F32)
    base = (lax.broadcasted_iota(jnp.int32, (tp, 1), 0) * 256).astype(F32)
    for t in range(own_rows // 128):
        part = hot[:, t * 128 : (t + 1) * 128]
        rank = jnp.dot(part.astype(BF16), before, preferred_element_type=F32) + carry
        rank = rank + jnp.where(rank >= half, 128.0 - half, 0.0)
        code[:, t * 128 : (t + 1) * 128] = jnp.sum(
            part * (rank + base), axis=0, keepdims=True
        ).astype(jnp.int32)
        carry = carry + jnp.sum(part, axis=1, keepdims=True)
    which = lax.broadcasted_iota(jnp.int32, (16, own_rows), 0)
    idrows[...] = jnp.where(
        which == 0, (local >> 7).astype(F32),
        jnp.where(which == 1, (local & 127).astype(F32), jnp.where(which == 2, 1.0, 0.0)),
    ).astype(BF16)
    uacc[...] = jnp.zeros_like(uacc)

    pl.semaphore_wait(barrier, tp - 1)

    def b_z(i):
        return remote(b_ref, bfull.at[me], bzs.at[i - 1], bzr.at[i - 1], lax.rem(me + 4 * i, tp))

    def b_y(i):
        blk = lax.rem(me + 4 * nz - 4 * i, tp)
        return remote(bfull.at[blk], bfull.at[blk], bys.at[i], byr.at[i], ypeer)

    def b_c(i, other):
        blk = lax.rem(me + 4 * nz - 4 * i, tp)
        if other:
            blk = blk + 2 - 4 * y
        k = i + other * nz
        return remote(bfull.at[blk], bfull.at[blk], bcs.at[k], bcr.at[k], sib)

    bfull[me] = b_ref[...]
    for i in range(1, nz):
        b_z(i).start()
    b_y(0).start()
    b_c(0, 0).start()

    def core_copy(j):
        return remote(c_send.at[j], c_recv.at[j], cs.at[j], cr.at[j], sib)

    def y_copy(j):
        return remote(y_send.at[j], y_recv.at[j], ys.at[j], yr.at[j], ypeer)

    def z_copy(j, i):
        to = lax.rem(z + i, nz)
        return remote(
            z_send.at[j, to], z_recv.at[j, i - 1], zs.at[j, i - 1], zr.at[j, i - 1],
            lax.rem(me + 4 * i, tp),
        )

    def a_copy(i):
        to = lax.rem(me + i, tp)
        return remote(abuf.at[to], got.at[i], as_.at[i], ar.at[i], to)

    def t_copy(i):
        to = lax.rem(me + i, tp)
        blk = (to % 2) * nb + ((to // 2) % 2) * nz + to // 4
        return remote(tsend.at[blk], trecv.at[i], ts.at[i], tr.at[i], to)

    lane = lax.broadcasted_iota(jnp.int32, (hp, 128), 1)
    per = 2 * tp // n

    def send_rows(i):
        to = lax.rem(me + i, tp)
        spot = jnp.where(
            code[...] == to * 256 + lax.broadcasted_iota(jnp.int32, (256, own_rows), 0), 1.0, 0.0
        ).astype(BF16)
        picked = jnp.dot(spot, aa_ref[...], preferred_element_type=F32)
        rows_out = jnp.where(lane < 64, picked[:hp], picked[128 : 128 + hp])
        marks = lax.dot_general(idrows[...], spot, NT, preferred_element_type=F32)
        block = jnp.concatenate([rows_out, marks[:8, :128], marks[:8, 128:]], axis=0).astype(BF16)

        @pl.when(i > 0)
        def _():
            abuf[to] = block
            a_copy(i).start()

        @pl.when(i == 0)
        def _():
            got[0] = block

    def use_rows(i):
        @pl.when(i > 0)
        def _():
            a_copy(i).wait_recv()

        block = got[i]
        marks = block[hp:].astype(F32)
        found = []
        for h in range(2):
            m = marks[8 * h : 8 * h + 8]
            row = jnp.where(m[2:3] > 0.5, m[0:1] * 128.0 + m[1:2], -1.0).astype(jnp.int32)
            found.append(row)
        row = jnp.concatenate(found, axis=1)
        spot = jnp.where(
            row == lax.broadcasted_iota(jnp.int32, (own_rows, 256), 0), 1.0, 0.0
        ).astype(BF16)
        lq = jnp.dot(late[...], spot, preferred_element_type=F32).astype(BF16)
        k = hp + 16
        for h in range(2):
            uacc[h] += jnp.dot(lq[:, 128 * h : 128 * h + k], block, preferred_element_type=F32)

    @pl.loop(0, n + 5)
    def _(s):
        @pl.when(s < n)
        def _():
            @pl.when(s + W_SLOTS - 1 < n)
            def _():
                for copy in w_copies(s + W_SLOTS - 1):
                    copy.start()

            for copy in w_copies(s):
                copy.wait()
            slot, ps = lax.rem(s, W_SLOTS), lax.rem(s, 2)
            for h in range(2):
                r = jnp.dot(
                    late[...], wbuf[slot, :, h * cw : (h + 1) * cw], preferred_element_type=F32
                )
                pbuf[ps, :, h * rows : (h + 1) * rows, :] = r.reshape(tp, rows, cw)
            c_send[s] = pbuf[ps, pl.ds((1 - c) * nb, nb)].astype(BF16)
            core_copy(s).start()

        @pl.when((s >= 1) & (s < n + 1))
        def _():
            j = s - 1
            ps = lax.rem(j, 2)
            core_copy(j).wait_recv()
            y_send[j] = (
                pbuf[ps, pl.ds(c * nb + (1 - y) * nz, nz)]
                + c_recv[j, pl.ds((1 - y) * nz, nz)].astype(F32)
            ).astype(BF16)
            y_copy(j).start()
            y_own[j] = pbuf[ps, pl.ds(c * nb + y * nz, nz)] + c_recv[
                j, pl.ds(y * nz, nz)
            ].astype(F32)

        @pl.when(s < n // 2)
        def _():
            @pl.loop(0, per)
            def _(k):
                send_rows(s * per + k)

        @pl.when((s >= n // 2) & (s < n))
        def _():
            @pl.loop(0, per)
            def _(k):
                use_rows((s - n // 2) * per + k)

        @pl.when(s == 1)
        def _():
            for i in range(1, nz):
                b_z(i).wait_recv()
                b_y(i).start()
                b_c(i, 0).start()

        @pl.when(s == 3)
        def _():
            for i in range(nz):
                b_y(i).wait_recv()
                b_c(i, 1).start()

        @pl.when(s == n - 1)
        def _():
            low = uacc[0][:, :64] + uacc[1][:, 64:]
            low = jnp.concatenate([low, jnp.zeros_like(low)], axis=1)
            tsend[...] = low.reshape(tp, rows, 128)

            @pl.loop(1, tp)
            def _(i):
                t_copy(i).start()

        @pl.when((s >= 3) & (s < n + 3))
        def _():
            j = s - 3
            y_copy(j).wait_recv()
            total = y_own[j] + y_recv[j].astype(F32)
            z_send[j] = total.astype(BF16)
            for i in range(1, nz):
                z_copy(j, i).start()
            y_own[j] = total

        @pl.when(s >= 5)
        def _():
            j = s - 5
            total = y_own[j, z]
            for i in range(1, nz):
                z_copy(j, i).wait_recv()
                total = total + z_recv[j, i - 1].astype(F32)
            stream[:, pl.ds(pl.multiple_of(j * cw, 128), cw)] = total

    @pl.loop(1, tp)
    def _(i):
        t_copy(i).wait_recv()

    low = tsend[c * nb + y * nz + z]
    for i in range(1, tp):
        low = low + trecv[i]
    low = (low[:, :64] * adapter_scale).astype(BF16)
    for i in range(nz):
        b_c(i, 0).wait_recv()
        b_c(i, 1).wait_recv()
    bw = d_model // tp
    square = jnp.zeros((rows, 1), F32)
    for k in range(tp):
        h, at = (k * bw) // hd, (k * bw) % hd
        v = stream[h * rows : (h + 1) * rows, at : at + bw]
        v = v + res_ref[:, k * bw : (k + 1) * bw].astype(F32)
        v = v + jnp.dot(low, bfull[k], preferred_element_type=F32)
        stream[h * rows : (h + 1) * rows, at : at + bw] = v
        square = square + jnp.sum(v * v, axis=1, keepdims=True)
    inverse = lax.rsqrt(square * (1.0 / d_model) + norm_eps)

    pw = hd // PIECES

    def piece(ref, p):
        return ref.at[:, pl.ds(p * pw, pw)]

    def g_own(p):
        return pltpu.make_async_copy(piece(nbuf, p), piece(out_hbm.at[me], p), loc.at[p])

    def g_z(p, i):
        return remote(
            piece(nbuf, p), piece(out_hbm.at[me], p), gzs.at[p, i - 1], gzr.at[p, i - 1],
            lax.rem(me + 4 * i, tp),
        )

    def g_blk(i):
        return lax.rem(me + 4 * nz - 4 * i, tp)

    def g_y(p, i):
        dst = piece(out_hbm.at[g_blk(i)], p)
        src = piece(nbuf, p) if i == 0 else dst
        return remote(src, dst, gys.at[p, i], gyr.at[p, i], ypeer)

    def g_c(p, i, other):
        blk = g_blk(i) + (2 - 4 * y if other else 0)
        dst = piece(out_hbm.at[blk], p)
        src = piece(nbuf, p) if (i == 0 and not other) else dst
        k = i + other * nz
        return remote(src, dst, gcs.at[p, k], gcr.at[p, k], sib)

    for p in range(PIECES):
        v = []
        for h in range(2):
            v.append(
                stream[h * rows : (h + 1) * rows, p * pw : (p + 1) * pw]
                * inverse
                * gain_ref[h : h + 1, p * pw : (p + 1) * pw]
            )
        nbuf[:, p * pw : (p + 1) * pw] = jnp.concatenate(v, axis=0).astype(BF16)
        g_y(p, 0).start()
        for i in range(1, nz):
            g_z(p, i).start()
        g_c(p, 0, 0).start()
        g_own(p).start()

    items = [(p, i) for p in range(PIECES) for i in range(nz)]
    lag = nz
    for q in range(len(items) + lag):
        if q < len(items):
            p, i = items[q]
            if i > 0:
                g_z(p, i).wait_recv()
                g_y(p, i).start()
                g_c(p, i, 0).start()
        if q >= lag:
            p, i = items[q - lag]
            g_y(p, i).wait_recv()
            g_c(p, i, 1).start()

    for p in range(PIECES):
        g_own(p).wait()
        for i in range(nz):
            g_c(p, i, 0).wait()
            g_c(p, i, 1).wait()
            g_y(p, i).wait_send()
            if i > 0:
                g_z(p, i).wait_send()
    for i in range(nz):
        b_y(i).wait_send()
        b_c(i, 0).wait_send()
        b_c(i, 1).wait_send()
        if i > 0:
            b_z(i).wait_send()

    @pl.loop(1, tp)
    def _(i):
        a_copy(i).wait_send()
        t_copy(i).wait_send()

    @pl.loop(0, n)
    def _(j):
        core_copy(j).wait_send()
        y_copy(j).wait_send()
        for i in range(1, nz):
            z_copy(j, i).wait_send()


def on_device(
    hidden, positions, adapter_rows, adapter_a, adapter_b, frozen_down_weight, residual, gain
):
    tp = lax.axis_size("tp")
    nz = tp // 4
    rows, d_model = residual.shape
    own_rows = frozen_down_weight.shape[0]
    tokens = rows * tp
    half = own_rows // tp
    hp = (half + 15) // 16 * 16
    hd = d_model // 2
    cw = hd // CHUNKS
    order = positions.reshape(nz, 2, 2, rows).transpose(2, 1, 0, 3).reshape(tokens, 1)
    doubled = jnp.concatenate([adapter_a, adapter_a], axis=1)
    n = CHUNKS
    dma = pltpu.SemaphoreType.DMA
    blk = (2 * rows, cw)
    scratch = [
        pltpu.VMEM((W_SLOTS, own_rows, 2 * cw), BF16),
        pltpu.VMEM((tokens, own_rows), BF16),
        pltpu.VMEM((1, own_rows), jnp.int32),
        pltpu.VMEM((16, own_rows), BF16),
        pltpu.VMEM((tp, hp + 16, 128), BF16),
        pltpu.VMEM((tp, hp + 16, 128), BF16),
        pltpu.VMEM((2, tokens, 128), F32),
        pltpu.VMEM((tp, rows, 128), F32),
        pltpu.VMEM((tp, rows, 128), F32),
        pltpu.VMEM((tp,) + adapter_b.shape, BF16),
        pltpu.VMEM((2, tp) + blk, F32),
        pltpu.VMEM((n, 2 * nz) + blk, BF16),
        pltpu.VMEM((n, 2 * nz) + blk, BF16),
        pltpu.VMEM((n, nz) + blk, BF16),
        pltpu.VMEM((n, nz) + blk, BF16),
        pltpu.VMEM((n, nz) + blk, F32),
        pltpu.VMEM((n, nz) + blk, BF16),
        pltpu.VMEM((n, nz - 1) + blk, BF16),
        pltpu.VMEM((2 * rows, hd), F32),
        pltpu.VMEM((2 * rows, hd), BF16),
        dma((W_SLOTS, 2)),
        dma((n,)), dma((n,)),
        dma((n,)), dma((n,)),
        dma((n, nz - 1)), dma((n, nz - 1)),
        dma((tp,)), dma((tp,)),
        dma((tp,)), dma((tp,)),
        dma((nz - 1,)), dma((nz - 1,)),
        dma((nz,)), dma((nz,)),
        dma((2 * nz,)), dma((2 * nz,)),
        dma((PIECES, nz - 1)), dma((PIECES, nz - 1)),
        dma((PIECES, nz)), dma((PIECES, nz)),
        dma((PIECES, 2 * nz)), dma((PIECES, 2 * nz)),
        dma((PIECES,)),
    ]
    vmem = pl.BlockSpec(memory_space=pltpu.VMEM)
    hbm = pl.BlockSpec(memory_space=pl.ANY)
    cfg = (tp, nz, rows, tokens, half, hp, own_rows, d_model)
    blocks = pl.pallas_call(
        functools.partial(kernel, cfg),
        out_shape=jax.ShapeDtypeStruct((tp, 2 * rows, hd), BF16),
        in_specs=[vmem, vmem, vmem, vmem, vmem, hbm, vmem, vmem],
        out_specs=hbm,
        scratch_shapes=scratch,
        compiler_params=pltpu.CompilerParams(
            collective_id=0, has_side_effects=True, vmem_limit_bytes=62 * 1024 * 1024
        ),
        cost_estimate=pl.CostEstimate(
            flops=2 * tokens * own_rows * d_model,
            bytes_accessed=2 * own_rows * d_model,
            transcendentals=0,
        ),
    )(
        order, hidden, adapter_rows.reshape(1, own_rows), doubled, adapter_b,
        frozen_down_weight, residual, gain.astype(F32).reshape(2, hd),
    )
    return blocks.reshape(tp, 2, rows, hd).transpose(0, 2, 1, 3).reshape(tokens, d_model)


def solution(mesh):
    placed = (
        P("groups", "tp"),
        P("groups"),
        P("tp"),
        P("tp", None),
        P(None, "tp"),
        P("tp", None),
        P(("groups", "tp"), None),
        P(),
    )
    return jax.shard_map(
        on_device, mesh=mesh, in_specs=placed, out_specs=P("groups", None), check_vma=False
    )
```

time: 262 us -> 145 us (0.55); the launches traced: 258 us -> 144 us
  waiting for transfers between devices: 154 us -> 0 us
  Pallas kernels: 0 us -> 116 us
  matrix products: 26 us -> 0 us
  local copies, waits for them, and re-layouts: 42.4 us -> 27.3 us
  between operations: 13.2 us -> 0.04 us
  starting transfers between devices: 12.4 us -> 0 us
  other arithmetic: 10.4 us -> 1.03 us
    pallas_call x0 -> x1, Pallas kernels: none -> 116 us  [on_device(): pl.pallas_call(functools.partial(kernel, cfg), out_shape=jax.ShapeDtypeSt...]
    reduce_scatter x1 -> x0, waiting for transfers between devices: 83.1 us -> none  [on_device(): lax.psum_scatter(jnp.dot(late_rows, merged_weight, preferred_element_type...]
    all_gather x2 -> x0, waiting for transfers between devices: 61.3 us -> none  [the longest x1 61.3 us: on_device(): return lax.all_gather(normed, 'tp', axis=0, tiled=True)]
    scatter x3 -> x0, local copies, waits for them, and re-layouts: 26.5 us -> none  [the longest x1 10.1 us: on_device(): factor_a = jnp.zeros((own_rows, adapter_inner_rank), adapter_a.dtype).at[...]
    dot_general x1 -> x0, matrix products: 26 us -> none  [on_device(): jnp.dot(late_rows, merged_weight, preferred_element_type=jnp.float32)]
    all_to_all x2 -> x0, starting transfers between devices: 12.3 us -> none  [the longest x1 6.33 us: on_device(): lax.all_to_all(send_ids, 'tp', split_axis=0, concat_axis=0, tiled=True)]
    transpose x0 -> x2, local copies, waits for them, and re-layouts: none -> 12.1 us  [the longest x1 12.1 us: on_device(): blocks.reshape(tp, 2, rows, hd).transpose(0, 2, 1, 3)]
    all_to_all x2 -> x0, waiting for transfers between devices: 8.71 us -> none  [the longest x1 8.7 us: on_device(): lax.all_to_all(send_rows, 'tp', split_axis=0, concat_axis=0, tiled=True)]
  transfers between devices with their start and end apart: 5 -> 0, of which waited for: 3 -> 0; matrix products, arithmetic and copies ran while one was open for 16% -> 0% of each run, Pallas kernels for 0% -> 0%
where the time goes in v1:
time: 145 us; the launch traced here: 144 us
  Pallas kernels  116 us (80%)
  local copies, waits for them, and re-layouts  27.3 us (19%)
    pallas_call x1, Pallas kernels, on_device(): pl.pallas_call(functools.partial(kernel, cfg), out_shape=jax.ShapeDtypeSt...  116 us
    transpose x1, local copies, waits for them, and re-layouts, on_device(): blocks.reshape(tp, 2, rows, hd).transpose(0, 2, 1, 3)  12.1 us
    unnamed x2, local copies, waits for them, and re-layouts  11.1 us

profile of v1, /device:TPU:29, one launch (start us, length us, event | category | flops | bytes accessed | tf_op | source)
XLA Modules:
  0.0 144.2 jit_solution(11513528728322711459)
XLA Ops:
  0.0 1.3 reshape.22.ids_ref
  1.3 0.8 reshape.20
  2.1 1.3 reshape.28.gain_ref
  3.4 0.8 reshape.29.pos_ref
  4.2 1.2 copy.13
  5.4 1.0 pad_maximum_fusion.aa_ref
  6.5 115.8 %shard_map.82 = bf16[16,48,4096]{2,1,0:T(8,128)(2,1)} custom-call(s32[384,1]{1,0:T(8,128)} %reshape.29.pos_ref, bf16[768,1792]{1,0:T(8,128)(2,1)} %hidden_ref.1, s32[1,1792]{1,0:T(1,128)} %reshape.22.ids_ref, bf16[1792,128]{1,0:T(8,128)(2,1)} %pad_maximum_fusion.aa_ref, bf16[64,512]{1,0:T(8,128)(2,1)} %b_ref.1, bf16[1792,8192]{1,0:T(8,128)(2,1)} %w_hbm.1, ...), custom_call_target="tpu_custom_call" | custom-call | flops 11274289152 | bytes 29360128 | tf_op jit(solution)/shard_map/pallas_call | solution.py:443
  122.3 12.1 %copy.16 = bf16[16,24,2,4096]{3,2,1,0:T(2,128)(2,1)S(1)} copy(bf16[16,24,2,4096]{3,1,2,0:T(8,128)(2,1)} %bitcast.8) | data formatting | bytes 12582912 | tf_op jit(solution)/shard_map/transpose | solution.py:461
  134.4 9.9 %copy.17 = bf16[48,8,2,4096]{3,1,2,0:T(8,128)(2,1)} copy(bf16[48,8,2,4096]{3,2,1,0:T(2,128)(2,1)S(1)} %bitcast.7) | data formatting | bytes 12582912
  (1 shorter events, 0.0 us)

commit v2 on v1

--- a/solution.py
+++ b/solution.py
@@ -19,18 +19,20 @@
 
 def kernel(
     cfg,
-    pos_ref, hidden_ref, ids_ref, aa_ref, b_ref, w_hbm, res_ref, gain_ref,
+    pos_ref, hidden_ref, ids_ref, a_ref, b_ref, w_hbm, res_ref,
     out_hbm,
-    wbuf, late, code, idrows, abuf, got, uacc, tsend, trecv, bfull,
+    wbuf, late, aa_ref, code, idrows, abuf, got, uacc, tsend, tcore, trecv, bfull,
     pbuf, c_send, c_recv, y_send, y_recv, y_own, z_send, z_recv, stream, nbuf,
     w_sem, cs, cr, ys, yr, zs, zr, as_, ar, ts, tr,
-    bzs, bzr, bys, byr, bcs, bcr, gzs, gzr, gys, gyr, gcs, gcr, loc,
+    bzs, bzr, bys, byr, bcs, bcr, bxs, bxr, axs, axr, tcs, tcr, gzs, gzr, gys, gyr, gcs, gcr, loc,
 ):
-    tp, nz, rows, tokens, half, hp, own_rows, d_model = cfg
+    tp, nz, rows, tokens, quarter, qp, held, own_rows, d_model = cfg
     n = CHUNKS
     hd = d_model // 2
     cw = hd // n
     me = lax.axis_index("tp")
+    group = lax.axis_index("groups")
+    side = group % 2
     z, y, c = me // 4, (me // 2) % 2, me % 2
     sib = me + 1 - 2 * c
     ypeer = me + 2 - 4 * y
@@ -40,6 +42,12 @@
         return pltpu.make_async_remote_copy(
             src_ref=src, dst_ref=dst, send_sem=send, recv_sem=recv,
             device_id={"tp": dev}, device_id_type=pl.DeviceIdType.MESH,
+        )
+
+    def across(src, dst, send, recv):
+        return pltpu.make_async_remote_copy(
+            src_ref=src, dst_ref=dst, send_sem=send, recv_sem=recv,
+            device_id={"groups": group + 1 - 2 * side}, device_id_type=pl.DeviceIdType.MESH,
         )
 
     def w_copies(j):
@@ -66,9 +74,23 @@
             device_id_type=pl.DeviceIdType.MESH,
         )
 
+    pl.semaphore_signal(
+        barrier, inc=1, device_id={"groups": group + 1 - 2 * side},
+        device_id_type=pl.DeviceIdType.MESH,
+    )
+
     buf_rows = hidden_ref.shape[0]
+    wanted = pos_ref[...].reshape(1, tokens)
     pick = jnp.where(
-        pos_ref[...] == lax.broadcasted_iota(jnp.int32, (tokens, buf_rows), 1), 1.0, 0.0
+        wanted == lax.broadcasted_iota(jnp.int32, (buf_rows, tokens), 0), 1.0, 0.0
+    )
+    pick = pick.T
+    pick = jnp.concatenate(
+        [
+            pick[(4 * i + 2 * j + k) * rows : (4 * i + 2 * j + k + 1) * rows]
+            for k in range(2) for j in range(2) for i in range(nz)
+        ],
+        axis=0,
     ).astype(BF16)
     lw = 256 if own_rows % 256 == 0 else 128
     for t in range(own_rows // lw):
@@ -76,49 +98,57 @@
             pick, hidden_ref[:, t * lw : (t + 1) * lw], preferred_element_type=F32
         ).astype(BF16)
 
-    ids = ids_ref[...]
-    first = lax.broadcasted_iota(jnp.int32, (tp, 1), 0) * own_rows
-    mine = (ids >= first) & (ids < first + own_rows)
-    hot = jnp.where(mine, 1.0, 0.0)
-    local = jnp.sum(jnp.where(mine, ids - first, 0), axis=0, keepdims=True)
-    before = jnp.where(
-        lax.broadcasted_iota(jnp.int32, (128, 128), 0)
-        < lax.broadcasted_iota(jnp.int32, (128, 128), 1), 1.0, 0.0,
-    ).astype(BF16)
-    carry = jnp.zeros((tp, 1), F32)
-    base = (lax.broadcasted_iota(jnp.int32, (tp, 1), 0) * 256).astype(F32)
-    for t in range(own_rows // 128):
-        part = hot[:, t * 128 : (t + 1) * 128]
-        rank = jnp.dot(part.astype(BF16), before, preferred_element_type=F32) + carry
-        rank = rank + jnp.where(rank >= half, 128.0 - half, 0.0)
-        code[:, t * 128 : (t + 1) * 128] = jnp.sum(
-            part * (rank + base), axis=0, keepdims=True
-        ).astype(jnp.int32)
-        carry = carry + jnp.sum(part, axis=1, keepdims=True)
-    which = lax.broadcasted_iota(jnp.int32, (16, own_rows), 0)
-    idrows[...] = jnp.where(
-        which == 0, (local >> 7).astype(F32),
-        jnp.where(which == 1, (local & 127).astype(F32), jnp.where(which == 2, 1.0, 0.0)),
-    ).astype(BF16)
     uacc[...] = jnp.zeros_like(uacc)
 
-    pl.semaphore_wait(barrier, tp - 1)
+    pl.semaphore_wait(barrier, tp)
+
+    def find_slots():
+        ids = ids_ref[...].reshape(1, own_rows)
+        aa_ref[...] = jnp.concatenate([a_ref[...], a_ref[...]], axis=0)
+        first = lax.broadcasted_iota(jnp.int32, (tp, 1), 0) * own_rows
+        mine = (ids >= first) & (ids < first + own_rows)
+        hot = jnp.where(mine, 1.0, 0.0)
+        local = jnp.sum(jnp.where(mine, ids - first, 0), axis=0, keepdims=True)
+        before = jnp.where(
+            lax.broadcasted_iota(jnp.int32, (128, 128), 0)
+            < lax.broadcasted_iota(jnp.int32, (128, 128), 1), 1.0, 0.0,
+        ).astype(BF16)
+        carry = jnp.zeros((tp, 1), F32) - (side * 2 * quarter).astype(F32)
+        base = (lax.broadcasted_iota(jnp.int32, (tp, 1), 0) * 128).astype(F32)
+        for t in range(own_rows // 128):
+            part = hot[:, t * 128 : (t + 1) * 128]
+            rank = jnp.dot(part.astype(BF16), before, preferred_element_type=F32) + carry
+            spot = rank + base + jnp.where(rank >= quarter, 64.0 - quarter, 0.0)
+            spot = jnp.where((rank >= 0.0) & (rank < 2.0 * quarter), spot, -1.0)
+            code[:, t * 128 : (t + 1) * 128] = jnp.sum(
+                part * spot, axis=0, keepdims=True
+            ).astype(jnp.int32)
+            carry = carry + jnp.sum(part, axis=1, keepdims=True)
+        which = lax.broadcasted_iota(jnp.int32, (16, own_rows), 0)
+        idrows[...] = jnp.where(
+            which == 0, (local >> 7).astype(F32),
+            jnp.where(which == 1, (local & 127).astype(F32), jnp.where(which == 2, 1.0, 0.0)),
+        ).astype(BF16)
 
     def b_z(i):
-        return remote(b_ref, bfull.at[me], bzs.at[i - 1], bzr.at[i - 1], lax.rem(me + 4 * i, tp))
+        return remote(bfull.at[me, side], bfull.at[me, side], bzs.at[i - 1], bzr.at[i - 1], lax.rem(me + 4 * i, tp))
 
     def b_y(i):
         blk = lax.rem(me + 4 * nz - 4 * i, tp)
-        return remote(bfull.at[blk], bfull.at[blk], bys.at[i], byr.at[i], ypeer)
+        return remote(bfull.at[blk, side], bfull.at[blk, side], bys.at[i], byr.at[i], ypeer)
 
     def b_c(i, other):
         blk = lax.rem(me + 4 * nz - 4 * i, tp)
         if other:
             blk = blk + 2 - 4 * y
         k = i + other * nz
-        return remote(bfull.at[blk], bfull.at[blk], bcs.at[k], bcr.at[k], sib)
-
-    bfull[me] = b_ref[...]
+        return remote(bfull.at[blk, side], bfull.at[blk, side], bcs.at[k], bcr.at[k], sib)
+
+    def b_x():
+        return across(bfull.at[:, side], bfull.at[:, side], bxs, bxr)
+
+    br = b_ref.shape[0] // 2
+    bfull[me, side] = b_ref[pl.ds(pl.multiple_of(side * br, 16), br), :]
     for i in range(1, nz):
         b_z(i).start()
     b_y(0).start()
@@ -139,25 +169,36 @@
 
     def a_copy(i):
         to = lax.rem(me + i, tp)
-        return remote(abuf.at[to], got.at[i], as_.at[i], ar.at[i], to)
+        return remote(abuf.at[to], got.at[i, side], as_.at[i], ar.at[i], to)
+
+    def a_x(i):
+        return across(got.at[i, side], got.at[i, side], axs.at[i], axr.at[i])
+
+    def t_core():
+        return remote(
+            tsend.at[pl.ds((1 - c) * nb, nb)], tcore, tcs, tcr, sib
+        )
 
     def t_copy(i):
-        to = lax.rem(me + i, tp)
-        blk = (to % 2) * nb + ((to // 2) % 2) * nz + to // 4
+        to = lax.rem(me + 2 * i, tp)
+        blk = c * nb + ((to // 2) % 2) * nz + to // 4
         return remote(tsend.at[blk], trecv.at[i], ts.at[i], tr.at[i], to)
 
-    lane = lax.broadcasted_iota(jnp.int32, (hp, 128), 1)
+    lane = lax.broadcasted_iota(jnp.int32, (qp, 128), 1)
     per = 2 * tp // n
 
     def send_rows(i):
         to = lax.rem(me + i, tp)
         spot = jnp.where(
-            code[...] == to * 256 + lax.broadcasted_iota(jnp.int32, (256, own_rows), 0), 1.0, 0.0
+            code[...] == to * 128 + lax.broadcasted_iota(jnp.int32, (128, own_rows), 0), 1.0, 0.0
         ).astype(BF16)
-        picked = jnp.dot(spot, aa_ref[...], preferred_element_type=F32)
-        rows_out = jnp.where(lane < 64, picked[:hp], picked[128 : 128 + hp])
+        picked = lax.dot_general(spot, aa_ref[...], NT, preferred_element_type=F32)
+        rows_out = jnp.where(lane < 64, picked[:qp], picked[64 : 64 + qp])
         marks = lax.dot_general(idrows[...], spot, NT, preferred_element_type=F32)
-        block = jnp.concatenate([rows_out, marks[:8, :128], marks[:8, 128:]], axis=0).astype(BF16)
+        parts = [rows_out, marks[:8]]
+        if held > qp + 8:
+            parts.append(jnp.zeros((held - qp - 8, 128), F32))
+        block = jnp.concatenate(parts, axis=0).astype(BF16)
 
         @pl.when(i > 0)
         def _():
@@ -166,28 +207,36 @@
 
         @pl.when(i == 0)
         def _():
-            got[0] = block
+            got[0, side] = block
+
+    def pass_rows(i):
+        @pl.when(i > 0)
+        def _():
+            a_copy(i).wait_recv()
+
+        a_x(i).start()
 
     def use_rows(i):
-        @pl.when(i > 0)
-        def _():
-            a_copy(i).wait_recv()
-
-        block = got[i]
-        marks = block[hp:].astype(F32)
+        a_x(i).wait_recv()
+        block = got[i].reshape(2 * held, 128)
         found = []
         for h in range(2):
-            m = marks[8 * h : 8 * h + 8]
-            row = jnp.where(m[2:3] > 0.5, m[0:1] * 128.0 + m[1:2], -1.0).astype(jnp.int32)
-            found.append(row)
-        row = jnp.concatenate(found, axis=1)
+            m = block[h * held + qp : h * held + qp + 8].astype(F32)
+            found.append(
+                jnp.where(m[2:3] > 0.5, m[0:1] * 128.0 + m[1:2], -1.0).astype(jnp.int32)
+            )
+        row = jnp.concatenate(
+            [found[0][:, :64], found[1][:, :64], found[0][:, 64:], found[1][:, 64:]], axis=1
+        )
         spot = jnp.where(
             row == lax.broadcasted_iota(jnp.int32, (own_rows, 256), 0), 1.0, 0.0
         ).astype(BF16)
         lq = jnp.dot(late[...], spot, preferred_element_type=F32).astype(BF16)
-        k = hp + 16
-        for h in range(2):
-            uacc[h] += jnp.dot(lq[:, 128 * h : 128 * h + k], block, preferred_element_type=F32)
+        for q in range(2):
+            part = lq[:, 128 * q : 128 * q + 128]
+            if held < 64:
+                part = jnp.concatenate([part[:, :held], part[:, 64 : 64 + held]], axis=1)
+            uacc[q] += jnp.dot(part, block, preferred_element_type=F32)
 
     @pl.loop(0, n + 5)
     def _(s):
@@ -223,11 +272,21 @@
                 j, pl.ds(y * nz, nz)
             ].astype(F32)
 
+        @pl.when(s == 0)
+        def _():
+            find_slots()
+
         @pl.when(s < n // 2)
         def _():
             @pl.loop(0, per)
             def _(k):
                 send_rows(s * per + k)
+
+        @pl.when((s >= 2) & (s < n // 2 + 2))
+        def _():
+            @pl.loop(0, per)
+            def _(k):
+                pass_rows((s - 2) * per + k)
 
         @pl.when((s >= n // 2) & (s < n))
         def _():
@@ -248,13 +307,27 @@
                 b_y(i).wait_recv()
                 b_c(i, 1).start()
 
+        @pl.when(s == 5)
+        def _():
+            for i in range(nz):
+                b_c(i, 0).wait_recv()
+                b_c(i, 1).wait_recv()
+            b_x().start()
+
         @pl.when(s == n - 1)
         def _():
             low = uacc[0][:, :64] + uacc[1][:, 64:]
             low = jnp.concatenate([low, jnp.zeros_like(low)], axis=1)
             tsend[...] = low.reshape(tp, rows, 128)
 
-            @pl.loop(1, tp)
+            t_core().start()
+
+        @pl.when(s == n)
+        def _():
+            t_core().wait()
+            tsend[pl.ds(c * nb, nb)] = tsend[pl.ds(c * nb, nb)] + tcore[...]
+
+            @pl.loop(1, tp // 2)
             def _(i):
                 t_copy(i).start()
 
@@ -277,29 +350,27 @@
                 total = total + z_recv[j, i - 1].astype(F32)
             stream[:, pl.ds(pl.multiple_of(j * cw, 128), cw)] = total
 
-    @pl.loop(1, tp)
+    @pl.loop(1, tp // 2)
     def _(i):
         t_copy(i).wait_recv()
 
     low = tsend[c * nb + y * nz + z]
-    for i in range(1, tp):
+    for i in range(1, tp // 2):
         low = low + trecv[i]
     low = (low[:, :64] * adapter_scale).astype(BF16)
-    for i in range(nz):
-        b_c(i, 0).wait_recv()
-        b_c(i, 1).wait_recv()
+    b_x().wait_recv()
     bw = d_model // tp
     square = jnp.zeros((rows, 1), F32)
     for k in range(tp):
         h, at = (k * bw) // hd, (k * bw) % hd
         v = stream[h * rows : (h + 1) * rows, at : at + bw]
         v = v + res_ref[:, k * bw : (k + 1) * bw].astype(F32)
-        v = v + jnp.dot(low, bfull[k], preferred_element_type=F32)
+        v = v + jnp.dot(low, bfull[k].reshape(2 * br, bw), preferred_element_type=F32)
         stream[h * rows : (h + 1) * rows, at : at + bw] = v
         square = square + jnp.sum(v * v, axis=1, keepdims=True)
     inverse = lax.rsqrt(square * (1.0 / d_model) + norm_eps)
 
-    pw = hd // PIECES
+    pw = d_model // PIECES
 
     def piece(ref, p):
         return ref.at[:, pl.ds(p * pw, pw)]
@@ -329,14 +400,10 @@
         return remote(src, dst, gcs.at[p, k], gcr.at[p, k], sib)
 
     for p in range(PIECES):
-        v = []
-        for h in range(2):
-            v.append(
-                stream[h * rows : (h + 1) * rows, p * pw : (p + 1) * pw]
-                * inverse
-                * gain_ref[h : h + 1, p * pw : (p + 1) * pw]
-            )
-        nbuf[:, p * pw : (p + 1) * pw] = jnp.concatenate(v, axis=0).astype(BF16)
+        h, at = (p * pw) // hd, (p * pw) % hd
+        nbuf[:, p * pw : (p + 1) * pw] = (
+            stream[h * rows : (h + 1) * rows, at : at + pw] * inverse
+        ).astype(BF16)
         g_y(p, 0).start()
         for i in range(1, nz):
             g_z(p, i).start()
@@ -375,7 +442,16 @@
     @pl.loop(1, tp)
     def _(i):
         a_copy(i).wait_send()
+
+    @pl.loop(1, tp // 2)
+    def _(i):
         t_copy(i).wait_send()
+
+    @pl.loop(0, tp)
+    def _(i):
+        a_x(i).wait_send()
+
+    b_x().wait_send()
 
     @pl.loop(0, n)
     def _(j):
@@ -393,26 +469,27 @@
     rows, d_model = residual.shape
     own_rows = frozen_down_weight.shape[0]
     tokens = rows * tp
-    half = own_rows // tp
-    hp = (half + 15) // 16 * 16
+    quarter = -(-2 * own_rows // tp // 4)
+    qp = (quarter + 7) // 8 * 8
+    held = (qp + 8 + 15) // 16 * 16
     hd = d_model // 2
     cw = hd // CHUNKS
-    order = positions.reshape(nz, 2, 2, rows).transpose(2, 1, 0, 3).reshape(tokens, 1)
-    doubled = jnp.concatenate([adapter_a, adapter_a], axis=1)
     n = CHUNKS
     dma = pltpu.SemaphoreType.DMA
     blk = (2 * rows, cw)
     scratch = [
         pltpu.VMEM((W_SLOTS, own_rows, 2 * cw), BF16),
         pltpu.VMEM((tokens, own_rows), BF16),
+        pltpu.VMEM((128, own_rows), BF16),
         pltpu.VMEM((1, own_rows), jnp.int32),
         pltpu.VMEM((16, own_rows), BF16),
-        pltpu.VMEM((tp, hp + 16, 128), BF16),
-        pltpu.VMEM((tp, hp + 16, 128), BF16),
+        pltpu.VMEM((tp, held, 128), BF16),
+        pltpu.VMEM((tp, 2, held, 128), BF16),
         pltpu.VMEM((2, tokens, 128), F32),
         pltpu.VMEM((tp, rows, 128), F32),
-        pltpu.VMEM((tp, rows, 128), F32),
-        pltpu.VMEM((tp,) + adapter_b.shape, BF16),
+        pltpu.VMEM((tp // 2, rows, 128), F32),
+        pltpu.VMEM((tp // 2, rows, 128), F32),
+        pltpu.VMEM((tp, 2, adapter_b.shape[0] // 2, adapter_b.shape[1]), BF16),
         pltpu.VMEM((2, tp) + blk, F32),
         pltpu.VMEM((n, 2 * nz) + blk, BF16),
         pltpu.VMEM((n, 2 * nz) + blk, BF16),
@@ -422,7 +499,7 @@
         pltpu.VMEM((n, nz) + blk, BF16),
         pltpu.VMEM((n, nz - 1) + blk, BF16),
         pltpu.VMEM((2 * rows, hd), F32),
-        pltpu.VMEM((2 * rows, hd), BF16),
+        pltpu.VMEM((rows, d_model), BF16),
         dma((W_SLOTS, 2)),
         dma((n,)), dma((n,)),
         dma((n,)), dma((n,)),
@@ -432,22 +509,25 @@
         dma((nz - 1,)), dma((nz - 1,)),
         dma((nz,)), dma((nz,)),
         dma((2 * nz,)), dma((2 * nz,)),
+        dma, dma, dma((tp,)), dma((tp,)), dma, dma,
         dma((PIECES, nz - 1)), dma((PIECES, nz - 1)),
         dma((PIECES, nz)), dma((PIECES, nz)),
         dma((PIECES, 2 * nz)), dma((PIECES, 2 * nz)),
         dma((PIECES,)),
     ]
     vmem = pl.BlockSpec(memory_space=pltpu.VMEM)
+    small = 2 * tokens * d_model <= 8 * 1024 * 1024
+    shape = (tp, rows, d_model)
     hbm = pl.BlockSpec(memory_space=pl.ANY)
-    cfg = (tp, nz, rows, tokens, half, hp, own_rows, d_model)
+    cfg = (tp, nz, rows, tokens, quarter, qp, held, own_rows, d_model)
     blocks = pl.pallas_call(
         functools.partial(kernel, cfg),
-        out_shape=jax.ShapeDtypeStruct((tp, 2 * rows, hd), BF16),
-        in_specs=[vmem, vmem, vmem, vmem, vmem, hbm, vmem, vmem],
-        out_specs=hbm,
+        out_shape=pltpu.VMEM(shape, BF16) if small else jax.ShapeDtypeStruct(shape, BF16),
+        in_specs=[vmem, vmem, vmem, vmem, vmem, hbm, vmem],
+        out_specs=vmem if small else hbm,
         scratch_shapes=scratch,
         compiler_params=pltpu.CompilerParams(
-            collective_id=0, has_side_effects=True, vmem_limit_bytes=62 * 1024 * 1024
+            collective_id=0, has_side_effects=True, vmem_limit_bytes=(52 if small else 62) * 1024 * 1024
         ),
         cost_estimate=pl.CostEstimate(
             flops=2 * tokens * own_rows * d_model,
@@ -455,10 +535,10 @@
             transcendentals=0,
         ),
     )(
-        order, hidden, adapter_rows.reshape(1, own_rows), doubled, adapter_b,
-        frozen_down_weight, residual, gain.astype(F32).reshape(2, hd),
+        positions, hidden, adapter_rows, adapter_a.T, adapter_b, frozen_down_weight, residual,
     )
-    return blocks.reshape(tp, 2, rows, hd).transpose(0, 2, 1, 3).reshape(tokens, d_model)
+    scaled = blocks.reshape(tokens, d_model).astype(F32) * gain.astype(F32)
+    return scaled.astype(BF16)
 
 
 def solution(mesh):

time: 145 us -> 119 us (0.82)
  local copies, waits for them, and re-layouts: 27.3 us -> 0 us
  other arithmetic: 1.03 us -> 5.39 us
  Pallas kernels: 116 us -> 113 us
    transpose x2 -> x0, local copies, waits for them, and re-layouts: 12.1 us -> none  [the longest x1 12.1 us: on_device(): blocks.reshape(tp, 2, rows, hd).transpose(0, 2, 1, 3)]
    unnamed x2 -> x0, local copies, waits for them, and re-layouts: 11.1 us -> none
    convert_element_type x0 -> x2, other arithmetic: none -> 5.39 us  [the longest x1 4.67 us: on_device(): return scaled.astype(BF16)]
    reshape x4 -> x0, local copies, waits for them, and re-layouts: 4.2 us -> none  [the longest x2 1.57 us: on_device(): positions.reshape(nz, 2, 2, rows).transpose(2, 1, 0, 3).reshape(tokens, 1)]
    pallas_call x1, Pallas kernels: 116 us -> 113 us  [on_device(): pl.pallas_call(functools.partial(kernel, cfg), out_shape=pltpu.VMEM(shape...]
where the time goes in v2:
time: 119 us; the launch traced here: 118 us
  Pallas kernels  113 us (95%)
  other arithmetic  5.39 us (5%)
    pallas_call x1, Pallas kernels, on_device(): pl.pallas_call(functools.partial(kernel, cfg), out_shape=pltpu.VMEM(shape...  113 us
    convert_element_type x1, other arithmetic, on_device(): return scaled.astype(BF16)  4.67 us

profile of v2, /device:TPU:29, one launch (start us, length us, event | category | flops | bytes accessed | tf_op | source)
XLA Modules:
  0.0 118.4 jit_solution(9313284962233819717)
XLA Ops:
  0.0 0.7 convert_element_type.14
  0.7 113.0 %shard_map.82 = bf16[16,24,8192]{2,1,0:T(8,128)(2,1)S(1)} custom-call(s32[384]{0:T(512)} %pos_ref.1, bf16[768,1792]{1,0:T(8,128)(2,1)} %hidden_ref.1, s32[1792]{0:T(1024)} %ids_ref.1, bf16[64,1792]{1,0:T(8,128)(2,1)} %bitcast.4, bf16[64,512]{1,0:T(8,128)(2,1)} %b_ref.1, bf16[1792,8192]{1,0:T(8,128)(2,1)} %w_hbm.1, bf16[24,8192]{1,0:T(8,128)(2,1)} %res_ref.1), custom_call_target="tpu_custom_call" | custom-call | flops 11274289152 | bytes 29360128 | tf_op jit(solution)/shard_map/pallas_call | solution.py:523
  113.7 4.7 %fusion = bf16[384,8192]{1,0:T(8,128)(2,1)} fusion(bf16[16,24,8192]{2,1,0:T(8,128)(2,1)S(1)} %shard_map.82, f32[8192]{0:T(1024)S(1)} %convert_element_type.14), kind=kLoop, calls=%fused_computation.1 | loop fusion | flops 9437184 | bytes 12615680 | tf_op jit(solution)/shard_map/convert_element_type | solution.py:541

commit v3 on v2

--- a/solution.py
+++ b/solution.py
@@ -185,7 +185,7 @@
         return remote(tsend.at[blk], trecv.at[i], ts.at[i], tr.at[i], to)
 
     lane = lax.broadcasted_iota(jnp.int32, (qp, 128), 1)
-    per = 2 * tp // n
+    per = tp // n
 
     def send_rows(i):
         to = lax.rem(me + i, tp)
@@ -276,23 +276,17 @@
         def _():
             find_slots()
 
-        @pl.when(s < n // 2)
+        @pl.when(s < n)
         def _():
             @pl.loop(0, per)
             def _(k):
                 send_rows(s * per + k)
 
-        @pl.when((s >= 2) & (s < n // 2 + 2))
+        @pl.when((s >= 2) & (s < n + 2))
         def _():
             @pl.loop(0, per)
             def _(k):
                 pass_rows((s - 2) * per + k)
-
-        @pl.when((s >= n // 2) & (s < n))
-        def _():
-            @pl.loop(0, per)
-            def _(k):
-                use_rows((s - n // 2) * per + k)
 
         @pl.when(s == 1)
         def _():
@@ -314,15 +308,7 @@
                 b_c(i, 1).wait_recv()
             b_x().start()
 
-        @pl.when(s == n - 1)
-        def _():
-            low = uacc[0][:, :64] + uacc[1][:, 64:]
-            low = jnp.concatenate([low, jnp.zeros_like(low)], axis=1)
-            tsend[...] = low.reshape(tp, rows, 128)
-
-            t_core().start()
-
-        @pl.when(s == n)
+        @pl.when(s == n + 3)
         def _():
             t_core().wait()
             tsend[pl.ds(c * nb, nb)] = tsend[pl.ds(c * nb, nb)] + tcore[...]
@@ -349,6 +335,20 @@
                 z_copy(j, i).wait_recv()
                 total = total + z_recv[j, i - 1].astype(F32)
             stream[:, pl.ds(pl.multiple_of(j * cw, 128), cw)] = total
+
+        @pl.when((s >= n - 1) & (s < n + 3))
+        def _():
+            @pl.loop(0, 2 * per)
+            def _(k):
+                use_rows((s - n + 1) * 2 * per + k)
+
+        @pl.when(s == n + 2)
+        def _():
+            low = uacc[0][:, :64] + uacc[1][:, 64:]
+            low = jnp.concatenate([low, jnp.zeros_like(low)], axis=1)
+            tsend[...] = low.reshape(tp, rows, 128)
+
+            t_core().start()
 
     @pl.loop(1, tp // 2)
     def _(i):

time: 119 us -> 117 us (0.983)
  Pallas kernels: 113 us -> 110 us
    pallas_call x1, Pallas kernels: 113 us -> 110 us  [on_device(): pl.pallas_call(functools.partial(kernel, cfg), out_shape=pltpu.VMEM(shape...]
where the time goes in v3:
time: 117 us; the launch traced here: 115 us
  Pallas kernels  110 us (94%)
  other arithmetic  5.39 us (5%)
    pallas_call x1, Pallas kernels, on_device(): pl.pallas_call(functools.partial(kernel, cfg), out_shape=pltpu.VMEM(shape...  110 us
    convert_element_type x1, other arithmetic, on_device(): return scaled.astype(BF16)  4.67 us

profile of v3, /device:TPU:29, one launch (start us, length us, event | category | flops | bytes accessed | tf_op | source)
XLA Modules:
  0.0 115.3 jit_solution(13371222628782600650)
XLA Ops:
  0.0 0.7 convert_element_type.14
  0.7 109.9 %shard_map.82 = bf16[16,24,8192]{2,1,0:T(8,128)(2,1)S(1)} custom-call(s32[384]{0:T(512)} %pos_ref.1, bf16[768,1792]{1,0:T(8,128)(2,1)} %hidden_ref.1, s32[1792]{0:T(1024)} %ids_ref.1, bf16[64,1792]{1,0:T(8,128)(2,1)} %bitcast.4, bf16[64,512]{1,0:T(8,128)(2,1)} %b_ref.1, bf16[1792,8192]{1,0:T(8,128)(2,1)} %w_hbm.1, bf16[24,8192]{1,0:T(8,128)(2,1)} %res_ref.1), custom_call_target="tpu_custom_call" | custom-call | flops 11274289152 | bytes 29360128 | tf_op jit(solution)/shard_map/pallas_call | solution.py:523
  110.6 4.7 %fusion = bf16[384,8192]{1,0:T(8,128)(2,1)} fusion(bf16[16,24,8192]{2,1,0:T(8,128)(2,1)S(1)} %shard_map.82, f32[8192]{0:T(1024)S(1)} %convert_element_type.14), kind=kLoop, calls=%fused_computation.1 | loop fusion | flops 9437184 | bytes 12615680 | tf_op jit(solution)/shard_map/convert_element_type | solution.py:541
